TPU v7x, 512 devices: a whole 4x8x8 slice. The times are simulated.
512 devices in a mesh: pipe: 8 (over z), ctx: 64 (over y, x, core).
Axes of the slice: x: 4, y: 8, z: 8, core: 2. Of those that a mesh axis runs over, the one named last changes fastest.
Arguments:
- queries: bfloat16 [8, 8192, 1536], P('pipe', 'ctx'), may hold values from -54 to 54
- keys_values: bfloat16 [8, 8192, 2, 512], P('pipe', 'ctx'), may hold values from -54 to 54
Outputs:
- passed: bfloat16 [8, 8192, 1536], P('pipe', 'ctx')
All inputs are finite; a program needn't handle non-finite values.
Results may differ from a plain program's by a relative error of at most 0.006.
Values may be sent and summed in bfloat16 or wider, within the bound.
A program may use at most 64 MiB of HBM per device.

v0:
```python
import math

import jax
import jax.numpy as jnp
from jax import lax
from jax.sharding import PartitionSpec as P

HD = 128
NSEQ = 2


NEG = -1e30


def passed_along(block, axis, distance):
    devices = range(lax.axis_size(axis))
    route = [((i - distance) % len(devices), i) for i in devices]
    return lax.ppermute(block, axis, route)


def attend(state, q_rows, keys, values, allowed, start):
    top_old, total_old, mixed_old = state
    count = q_rows.shape[0]
    scale = 1.0 / math.sqrt(q_rows.shape[-1])
    scores = jnp.einsum("qhgd,khd->hgqk", q_rows, keys, preferred_element_type=jnp.float32) * scale
    scores = jnp.where(allowed[None, None], scores, NEG)
    top_new = jnp.maximum(top_old, jnp.max(scores, axis=-1))
    weights = jnp.exp(scores - top_new[..., None])
    fade = jnp.exp(top_old - top_new)
    total_new = total_old * fade + jnp.sum(weights, axis=-1)
    mixed_new = mixed_old * fade[..., None] + jnp.einsum(
        "hgqk,khd->hgqd", weights.astype(jnp.bfloat16), values, preferred_element_type=jnp.float32
    )
    return (
        top_old.at[:, :, start : start + count].set(top_new),
        total_old.at[:, :, start : start + count].set(total_new),
        mixed_old.at[:, :, start : start + count].set(mixed_new),
    )


def ahead(block):
    return passed_along(block, "ctx", NSEQ)


def shards(queries, keys_values):
    rows = queries.shape[1]
    half = rows // 2
    kv_heads = keys_values.shape[-1] // HD
    q_heads = queries.shape[-1] // HD
    share = q_heads // kv_heads
    group = lax.axis_size("ctx") // NSEQ
    rank = lax.axis_index("ctx") // NSEQ
    grouped = queries[0].reshape(rows, kv_heads, share, HD)
    offsets = jnp.arange(half, dtype=jnp.int32)

    def positions(owner):
        return jnp.concatenate([owner * half + offsets, (2 * group - 1 - owner) * half + offsets])

    def split_block(block):
        return (block[:, 0].reshape(rows, kv_heads, HD), block[:, 1].reshape(rows, kv_heads, HD))

    mine = positions(rank)

    def remote(state, block, owner):
        keys, values = split_block(block)
        theirs = positions(owner)
        allowed = mine[:, None] >= theirs[None, :]
        return attend(state, grouped, keys, values, allowed, 0)

    state = (
        jnp.full((kv_heads, share, rows), NEG, jnp.float32),
        jnp.zeros((kv_heads, share, rows), jnp.float32),
        jnp.zeros((kv_heads, share, rows, HD), jnp.float32),
    )
    own = keys_values[0]
    own_keys, own_values = split_block(own)
    state = attend(state, grouped, own_keys, own_values, mine[:, None] >= mine[None, :], 0)

    def forward_step(step, carry):
        block, current = carry
        block = ahead(block)
        return (block, remote(current, block, (rank - step) % group))

    front, state = lax.fori_loop(1, group, forward_step, (own, state))
    top_fin, total_fin, mixed_fin = state
    result = mixed_fin / total_fin[..., None]
    result = result.transpose(2, 0, 1, 3).reshape(rows, q_heads * HD).astype(jnp.bfloat16)
    return passed_along(result[None], "pipe", 1)


def solution(mesh):
    placed = (P("pipe", "ctx", None), P("pipe", "ctx", None, None))
    return jax.shard_map(
        shards, mesh=mesh, in_specs=placed, out_specs=P("pipe", "ctx", None), check_vma=False
    )
```

profile of v0, /device:TPU:32, one launch (start us, length us, event | category | flops | bytes accessed | tf_op | source)
XLA Modules:
  0.0 434.1 jit_solution(18359560338523753913)
XLA Ops:
  3.7 412.4 %while.56 = (s32[]{:T(128)}, bf16[128,2,512]{0,2,1:T(8,128)(2,1)S(1)}, f32[4,3,128]{2,1,0:T(4,128)S(1)}, f32[4,3,128]{2,1,0:T(4,128)S(1)}, f32[4,3,128,128]{3,2,...) while((s32[]{:T(128)}, ...), condition=%wide.region_5.6_spmd.clone.clone, body=%wide.region_2.5_spmd.clone.clone.sunk | while | flops 102452496 | bytes 6818642 | solution.py:84
  3.7 3.4 collective-permute-start
  7.4 9.6 %collective-permute-done = bf16[128,2,512]{0,2,1:T(8,128)(2,1)S(1)} collective-permute-done((bf16[128,2,512]{0,2,1:T(8,128)(2,1)S(1)}, bf16[128,2,512]{0,2,1:T(8,128)(2,1)S(1)}, u32[]{:S(2)}, u32[]{:S(2)}) %collective-permute-start) | collective-permute-done | bytes 262176 | tf_op jit(solution)/shard_map/while/body/eval_jaxpr/ppermute | solution.py:18
  18.2 1.9 collective-permute-start
  20.3 10.3 %collective-permute-done = bf16[128,2,512]{0,2,1:T(8,128)(2,1)S(1)} collective-permute-done((bf16[128,2,512]{0,2,1:T(8,128)(2,1)S(1)}, bf16[128,2,512]{0,2,1:T(8,128)(2,1)S(1)}, u32[]{:S(2)}, u32[]{:S(2)}) %collective-permute-start) | collective-permute-done | bytes 262176 | tf_op jit(solution)/shard_map/while/body/eval_jaxpr/ppermute | solution.py:18
  33.8 9.5 %collective-permute-done = bf16[128,2,512]{0,2,1:T(8,128)(2,1)S(1)} collective-permute-done((bf16[128,2,512]{0,2,1:T(8,128)(2,1)S(1)}, bf16[128,2,512]{0,2,1:T(8,128)(2,1)S(1)}, u32[]{:S(2)}, u32[]{:S(2)}) %collective-permute-start) | collective-permute-done | bytes 262176 | tf_op jit(solution)/shard_map/while/body/eval_jaxpr/ppermute | solution.py:18
  44.4 1.9 collective-permute-start
  46.6 9.5 %collective-permute-done = bf16[128,2,512]{0,2,1:T(8,128)(2,1)S(1)} collective-permute-done((bf16[128,2,512]{0,2,1:T(8,128)(2,1)S(1)}, bf16[128,2,512]{0,2,1:T(8,128)(2,1)S(1)}, u32[]{:S(2)}, u32[]{:S(2)}) %collective-permute-start) | collective-permute-done | bytes 262176 | tf_op jit(solution)/shard_map/while/body/eval_jaxpr/ppermute | solution.py:18
  59.3 9.5 %collective-permute-done = bf16[128,2,512]{0,2,1:T(8,128)(2,1)S(1)} collective-permute-done((bf16[128,2,512]{0,2,1:T(8,128)(2,1)S(1)}, bf16[128,2,512]{0,2,1:T(8,128)(2,1)S(1)}, u32[]{:S(2)}, u32[]{:S(2)}) %collective-permute-start) | collective-permute-done | bytes 262176 | tf_op jit(solution)/shard_map/while/body/eval_jaxpr/ppermute | solution.py:18
  72.0 9.5 %collective-permute-done = bf16[128,2,512]{0,2,1:T(8,128)(2,1)S(1)} collective-permute-done((bf16[128,2,512]{0,2,1:T(8,128)(2,1)S(1)}, bf16[128,2,512]{0,2,1:T(8,128)(2,1)S(1)}, u32[]{:S(2)}, u32[]{:S(2)}) %collective-permute-start) | collective-permute-done | bytes 262176 | tf_op jit(solution)/shard_map/while/body/eval_jaxpr/ppermute | solution.py:18
  82.7 1.9 collective-permute-start
  84.8 9.5 %collective-permute-done = bf16[128,2,512]{0,2,1:T(8,128)(2,1)S(1)} collective-permute-done((bf16[128,2,512]{0,2,1:T(8,128)(2,1)S(1)}, bf16[128,2,512]{0,2,1:T(8,128)(2,1)S(1)}, u32[]{:S(2)}, u32[]{:S(2)}) %collective-permute-start) | collective-permute-done | bytes 262176 | tf_op jit(solution)/shard_map/while/body/eval_jaxpr/ppermute | solution.py:18
  97.5 9.5 %collective-permute-done = bf16[128,2,512]{0,2,1:T(8,128)(2,1)S(1)} collective-permute-done((bf16[128,2,512]{0,2,1:T(8,128)(2,1)S(1)}, bf16[128,2,512]{0,2,1:T(8,128)(2,1)S(1)}, u32[]{:S(2)}, u32[]{:S(2)}) %collective-permute-start) | collective-permute-done | bytes 262176 | tf_op jit(solution)/shard_map/while/body/eval_jaxpr/ppermute | solution.py:18
  110.3 10.5 %collective-permute-done = bf16[128,2,512]{0,2,1:T(8,128)(2,1)S(1)} collective-permute-done((bf16[128,2,512]{0,2,1:T(8,128)(2,1)S(1)}, bf16[128,2,512]{0,2,1:T(8,128)(2,1)S(1)}, u32[]{:S(2)}, u32[]{:S(2)}) %collective-permute-start) | collective-permute-done | bytes 262176 | tf_op jit(solution)/shard_map/while/body/eval_jaxpr/ppermute | solution.py:18
  121.9 1.9 collective-permute-start
  124.0 11.7 %collective-permute-done = bf16[128,2,512]{0,2,1:T(8,128)(2,1)S(1)} collective-permute-done((bf16[128,2,512]{0,2,1:T(8,128)(2,1)S(1)}, bf16[128,2,512]{0,2,1:T(8,128)(2,1)S(1)}, u32[]{:S(2)}, u32[]{:S(2)}) %collective-permute-start) | collective-permute-done | bytes 262176 | tf_op jit(solution)/shard_map/while/body/eval_jaxpr/ppermute | solution.py:18
  139.0 11.7 %collective-permute-done = bf16[128,2,512]{0,2,1:T(8,128)(2,1)S(1)} collective-permute-done((bf16[128,2,512]{0,2,1:T(8,128)(2,1)S(1)}, bf16[128,2,512]{0,2,1:T(8,128)(2,1)S(1)}, u32[]{:S(2)}, u32[]{:S(2)}) %collective-permute-start) | collective-permute-done | bytes 262176 | tf_op jit(solution)/shard_map/while/body/eval_jaxpr/ppermute | solution.py:18
  154.0 11.0 %collective-permute-done = bf16[128,2,512]{0,2,1:T(8,128)(2,1)S(1)} collective-permute-done((bf16[128,2,512]{0,2,1:T(8,128)(2,1)S(1)}, bf16[128,2,512]{0,2,1:T(8,128)(2,1)S(1)}, u32[]{:S(2)}, u32[]{:S(2)}) %collective-permute-start) | collective-permute-done | bytes 262176 | tf_op jit(solution)/shard_map/while/body/eval_jaxpr/ppermute | solution.py:18
  166.1 1.9 collective-permute-start
  168.2 10.1 %collective-permute-done = bf16[128,2,512]{0,2,1:T(8,128)(2,1)S(1)} collective-permute-done((bf16[128,2,512]{0,2,1:T(8,128)(2,1)S(1)}, bf16[128,2,512]{0,2,1:T(8,128)(2,1)S(1)}, u32[]{:S(2)}, u32[]{:S(2)}) %collective-permute-start) | collective-permute-done | bytes 262176 | tf_op jit(solution)/shard_map/while/body/eval_jaxpr/ppermute | solution.py:18
  179.4 1.9 collective-permute-start
  181.6 9.5 %collective-permute-done = bf16[128,2,512]{0,2,1:T(8,128)(2,1)S(1)} collective-permute-done((bf16[128,2,512]{0,2,1:T(8,128)(2,1)S(1)}, bf16[128,2,512]{0,2,1:T(8,128)(2,1)S(1)}, u32[]{:S(2)}, u32[]{:S(2)}) %collective-permute-start) | collective-permute-done | bytes 262176 | tf_op jit(solution)/shard_map/while/body/eval_jaxpr/ppermute | solution.py:18
  194.3 9.5 %collective-permute-done = bf16[128,2,512]{0,2,1:T(8,128)(2,1)S(1)} collective-permute-done((bf16[128,2,512]{0,2,1:T(8,128)(2,1)S(1)}, bf16[128,2,512]{0,2,1:T(8,128)(2,1)S(1)}, u32[]{:S(2)}, u32[]{:S(2)}) %collective-permute-start) | collective-permute-done | bytes 262176 | tf_op jit(solution)/shard_map/while/body/eval_jaxpr/ppermute | solution.py:18
  204.9 1.9 collective-permute-start
  207.0 9.5 %collective-permute-done = bf16[128,2,512]{0,2,1:T(8,128)(2,1)S(1)} collective-permute-done((bf16[128,2,512]{0,2,1:T(8,128)(2,1)S(1)}, bf16[128,2,512]{0,2,1:T(8,128)(2,1)S(1)}, u32[]{:S(2)}, u32[]{:S(2)}) %collective-permute-start) | collective-permute-done | bytes 262176 | tf_op jit(solution)/shard_map/while/body/eval_jaxpr/ppermute | solution.py:18
  219.8 9.5 %collective-permute-done = bf16[128,2,512]{0,2,1:T(8,128)(2,1)S(1)} collective-permute-done((bf16[128,2,512]{0,2,1:T(8,128)(2,1)S(1)}, bf16[128,2,512]{0,2,1:T(8,128)(2,1)S(1)}, u32[]{:S(2)}, u32[]{:S(2)}) %collective-permute-start) | collective-permute-done | bytes 262176 | tf_op jit(solution)/shard_map/while/body/eval_jaxpr/ppermute | solution.py:18
  232.5 9.5 %collective-permute-done = bf16[128,2,512]{0,2,1:T(8,128)(2,1)S(1)} collective-permute-done((bf16[128,2,512]{0,2,1:T(8,128)(2,1)S(1)}, bf16[128,2,512]{0,2,1:T(8,128)(2,1)S(1)}, u32[]{:S(2)}, u32[]{:S(2)}) %collective-permute-start) | collective-permute-done | bytes 262176 | tf_op jit(solution)/shard_map/while/body/eval_jaxpr/ppermute | solution.py:18
  243.1 1.9 collective-permute-start
  245.3 9.5 %collective-permute-done = bf16[128,2,512]{0,2,1:T(8,128)(2,1)S(1)} collective-permute-done((bf16[128,2,512]{0,2,1:T(8,128)(2,1)S(1)}, bf16[128,2,512]{0,2,1:T(8,128)(2,1)S(1)}, u32[]{:S(2)}, u32[]{:S(2)}) %collective-permute-start) | collective-permute-done | bytes 262176 | tf_op jit(solution)/shard_map/while/body/eval_jaxpr/ppermute | solution.py:18
  255.9 1.9 collective-permute-start
  258.1 10.6 %collective-permute-done = bf16[128,2,512]{0,2,1:T(8,128)(2,1)S(1)} collective-permute-done((bf16[128,2,512]{0,2,1:T(8,128)(2,1)S(1)}, bf16[128,2,512]{0,2,1:T(8,128)(2,1)S(1)}, u32[]{:S(2)}, u32[]{:S(2)}) %collective-permute-start) | collective-permute-done | bytes 262176 | tf_op jit(solution)/shard_map/while/body/eval_jaxpr/ppermute | solution.py:18
  271.9 11.8 %collective-permute-done = bf16[128,2,512]{0,2,1:T(8,128)(2,1)S(1)} collective-permute-done((bf16[128,2,512]{0,2,1:T(8,128)(2,1)S(1)}, bf16[128,2,512]{0,2,1:T(8,128)(2,1)S(1)}, u32[]{:S(2)}, u32[]{:S(2)}) %collective-permute-start) | collective-permute-done | bytes 262176 | tf_op jit(solution)/shard_map/while/body/eval_jaxpr/ppermute | solution.py:18
  284.9 1.9 collective-permute-start
  287.0 11.6 %collective-permute-done = bf16[128,2,512]{0,2,1:T(8,128)(2,1)S(1)} collective-permute-done((bf16[128,2,512]{0,2,1:T(8,128)(2,1)S(1)}, bf16[128,2,512]{0,2,1:T(8,128)(2,1)S(1)}, u32[]{:S(2)}, u32[]{:S(2)}) %collective-permute-start) | collective-permute-done | bytes 262176 | tf_op jit(solution)/shard_map/while/body/eval_jaxpr/ppermute | solution.py:18
  299.7 1.9 collective-permute-start
  301.9 10.8 %collective-permute-done = bf16[128,2,512]{0,2,1:T(8,128)(2,1)S(1)} collective-permute-done((bf16[128,2,512]{0,2,1:T(8,128)(2,1)S(1)}, bf16[128,2,512]{0,2,1:T(8,128)(2,1)S(1)}, u32[]{:S(2)}, u32[]{:S(2)}) %collective-permute-start) | collective-permute-done | bytes 262176 | tf_op jit(solution)/shard_map/while/body/eval_jaxpr/ppermute | solution.py:18
  315.9 9.8 %collective-permute-done = bf16[128,2,512]{0,2,1:T(8,128)(2,1)S(1)} collective-permute-done((bf16[128,2,512]{0,2,1:T(8,128)(2,1)S(1)}, bf16[128,2,512]{0,2,1:T(8,128)(2,1)S(1)}, u32[]{:S(2)}, u32[]{:S(2)}) %collective-permute-start) | collective-permute-done | bytes 262176 | tf_op jit(solution)/shard_map/while/body/eval_jaxpr/ppermute | solution.py:18
  329.0 9.5 %collective-permute-done = bf16[128,2,512]{0,2,1:T(8,128)(2,1)S(1)} collective-permute-done((bf16[128,2,512]{0,2,1:T(8,128)(2,1)S(1)}, bf16[128,2,512]{0,2,1:T(8,128)(2,1)S(1)}, u32[]{:S(2)}, u32[]{:S(2)}) %collective-permute-start) | collective-permute-done | bytes 262176 | tf_op jit(solution)/shard_map/while/body/eval_jaxpr/ppermute | solution.py:18
  339.7 1.9 collective-permute-start
  341.8 9.5 %collective-permute-done = bf16[128,2,512]{0,2,1:T(8,128)(2,1)S(1)} collective-permute-done((bf16[128,2,512]{0,2,1:T(8,128)(2,1)S(1)}, bf16[128,2,512]{0,2,1:T(8,128)(2,1)S(1)}, u32[]{:S(2)}, u32[]{:S(2)}) %collective-permute-start) | collective-permute-done | bytes 262176 | tf_op jit(solution)/shard_map/while/body/eval_jaxpr/ppermute | solution.py:18
  354.5 9.5 %collective-permute-done = bf16[128,2,512]{0,2,1:T(8,128)(2,1)S(1)} collective-permute-done((bf16[128,2,512]{0,2,1:T(8,128)(2,1)S(1)}, bf16[128,2,512]{0,2,1:T(8,128)(2,1)S(1)}, u32[]{:S(2)}, u32[]{:S(2)}) %collective-permute-start) | collective-permute-done | bytes 262176 | tf_op jit(solution)/shard_map/while/body/eval_jaxpr/ppermute | solution.py:18
  367.3 9.5 %collective-permute-done = bf16[128,2,512]{0,2,1:T(8,128)(2,1)S(1)} collective-permute-done((bf16[128,2,512]{0,2,1:T(8,128)(2,1)S(1)}, bf16[128,2,512]{0,2,1:T(8,128)(2,1)S(1)}, u32[]{:S(2)}, u32[]{:S(2)}) %collective-permute-start) | collective-permute-done | bytes 262176 | tf_op jit(solution)/shard_map/while/body/eval_jaxpr/ppermute | solution.py:18
  377.9 1.9 collective-permute-start
  380.0 9.5 %collective-permute-done = bf16[128,2,512]{0,2,1:T(8,128)(2,1)S(1)} collective-permute-done((bf16[128,2,512]{0,2,1:T(8,128)(2,1)S(1)}, bf16[128,2,512]{0,2,1:T(8,128)(2,1)S(1)}, u32[]{:S(2)}, u32[]{:S(2)}) %collective-permute-start) | collective-permute-done | bytes 262176 | tf_op jit(solution)/shard_map/while/body/eval_jaxpr/ppermute | solution.py:18
  392.7 9.5 %collective-permute-done = bf16[128,2,512]{0,2,1:T(8,128)(2,1)S(1)} collective-permute-done((bf16[128,2,512]{0,2,1:T(8,128)(2,1)S(1)}, bf16[128,2,512]{0,2,1:T(8,128)(2,1)S(1)}, u32[]{:S(2)}, u32[]{:S(2)}) %collective-permute-start) | collective-permute-done | bytes 262176 | tf_op jit(solution)/shard_map/while/body/eval_jaxpr/ppermute | solution.py:18
  405.5 9.5 %collective-permute-done = bf16[128,2,512]{0,2,1:T(8,128)(2,1)S(1)} collective-permute-done((bf16[128,2,512]{0,2,1:T(8,128)(2,1)S(1)}, bf16[128,2,512]{0,2,1:T(8,128)(2,1)S(1)}, u32[]{:S(2)}, u32[]{:S(2)}) %collective-permute-start) | collective-permute-done | bytes 262176 | tf_op jit(solution)/shard_map/while/body/eval_jaxpr/ppermute | solution.py:18
  416.5 4.3 collective-permute-start.1
  420.8 12.4 %collective-permute-done.1 = bf16[1,128,1536]{1,2,0:T(8,128)(2,1)S(1)} collective-permute-done((bf16[1,128,1536]{1,2,0:T(8,128)(2,1)S(1)}, bf16[1,128,1536]{1,2,0:T(8,128)(2,1)S(1)}, u32[]{:S(2)}, u32[]{:S(2)}) %collective-permute-start.1) | collective-permute-done | bytes 393248 | tf_op jit(solution)/shard_map/ppermute | solution.py:18
  (375 shorter events, 76.8 us)
Async XLA Ops:
  1.3 1.0 copy-start
  3.7 13.3 %collective-permute-start = (bf16[128,2,512]{0,2,1:T(8,128)(2,1)S(1)}, bf16[128,2,512]{0,2,1:T(8,128)(2,1)S(1)}, u32[]{:S(2)}, u32[]{:S(2)}) collective-permute-start(bf16[128,2,512]{0,2,1:T(8,128)(2,1)S(1)} %get-tuple-element.554), channel_id=1, source_target_pairs={{62,0},{63,1},{0,2},{1,3},{2,4},{3,5},{4,6},{5,7},{6,8},{7,9},{8,1... | collective-permute-start | bytes 786440 | tf_op jit(solution)/shard_map/while/body/eval_jaxpr/ppermute | solution.py:18
  18.2 12.4 %collective-permute-start = (bf16[128,2,512]{0,2,1:T(8,128)(2,1)S(1)}, bf16[128,2,512]{0,2,1:T(8,128)(2,1)S(1)}, u32[]{:S(2)}, u32[]{:S(2)}) collective-permute-start(bf16[128,2,512]{0,2,1:T(8,128)(2,1)S(1)} %get-tuple-element.554), channel_id=1, source_target_pairs={{62,0},{63,1},{0,2},{1,3},{2,4},{3,5},{4,6},{5,7},{6,8},{7,9},{8,1... | collective-permute-start | bytes 786440 | tf_op jit(solution)/shard_map/while/body/eval_jaxpr/ppermute | solution.py:18
  31.7 11.6 %collective-permute-start = (bf16[128,2,512]{0,2,1:T(8,128)(2,1)S(1)}, bf16[128,2,512]{0,2,1:T(8,128)(2,1)S(1)}, u32[]{:S(2)}, u32[]{:S(2)}) collective-permute-start(bf16[128,2,512]{0,2,1:T(8,128)(2,1)S(1)} %get-tuple-element.554), channel_id=1, source_target_pairs={{62,0},{63,1},{0,2},{1,3},{2,4},{3,5},{4,6},{5,7},{6,8},{7,9},{8,1... | collective-permute-start | bytes 786440 | tf_op jit(solution)/shard_map/while/body/eval_jaxpr/ppermute | solution.py:18
  44.4 11.6 %collective-permute-start = (bf16[128,2,512]{0,2,1:T(8,128)(2,1)S(1)}, bf16[128,2,512]{0,2,1:T(8,128)(2,1)S(1)}, u32[]{:S(2)}, u32[]{:S(2)}) collective-permute-start(bf16[128,2,512]{0,2,1:T(8,128)(2,1)S(1)} %get-tuple-element.554), channel_id=1, source_target_pairs={{62,0},{63,1},{0,2},{1,3},{2,4},{3,5},{4,6},{5,7},{6,8},{7,9},{8,1... | collective-permute-start | bytes 786440 | tf_op jit(solution)/shard_map/while/body/eval_jaxpr/ppermute | solution.py:18
  57.2 11.6 %collective-permute-start = (bf16[128,2,512]{0,2,1:T(8,128)(2,1)S(1)}, bf16[128,2,512]{0,2,1:T(8,128)(2,1)S(1)}, u32[]{:S(2)}, u32[]{:S(2)}) collective-permute-start(bf16[128,2,512]{0,2,1:T(8,128)(2,1)S(1)} %get-tuple-element.554), channel_id=1, source_target_pairs={{62,0},{63,1},{0,2},{1,3},{2,4},{3,5},{4,6},{5,7},{6,8},{7,9},{8,1... | collective-permute-start | bytes 786440 | tf_op jit(solution)/shard_map/while/body/eval_jaxpr/ppermute | solution.py:18
  69.9 11.6 %collective-permute-start = (bf16[128,2,512]{0,2,1:T(8,128)(2,1)S(1)}, bf16[128,2,512]{0,2,1:T(8,128)(2,1)S(1)}, u32[]{:S(2)}, u32[]{:S(2)}) collective-permute-start(bf16[128,2,512]{0,2,1:T(8,128)(2,1)S(1)} %get-tuple-element.554), channel_id=1, source_target_pairs={{62,0},{63,1},{0,2},{1,3},{2,4},{3,5},{4,6},{5,7},{6,8},{7,9},{8,1... | collective-permute-start | bytes 786440 | tf_op jit(solution)/shard_map/while/body/eval_jaxpr/ppermute | solution.py:18
  82.7 11.6 %collective-permute-start = (bf16[128,2,512]{0,2,1:T(8,128)(2,1)S(1)}, bf16[128,2,512]{0,2,1:T(8,128)(2,1)S(1)}, u32[]{:S(2)}, u32[]{:S(2)}) collective-permute-start(bf16[128,2,512]{0,2,1:T(8,128)(2,1)S(1)} %get-tuple-element.554), channel_id=1, source_target_pairs={{62,0},{63,1},{0,2},{1,3},{2,4},{3,5},{4,6},{5,7},{6,8},{7,9},{8,1... | collective-permute-start | bytes 786440 | tf_op jit(solution)/shard_map/while/body/eval_jaxpr/ppermute | solution.py:18
  95.4 11.6 %collective-permute-start = (bf16[128,2,512]{0,2,1:T(8,128)(2,1)S(1)}, bf16[128,2,512]{0,2,1:T(8,128)(2,1)S(1)}, u32[]{:S(2)}, u32[]{:S(2)}) collective-permute-start(bf16[128,2,512]{0,2,1:T(8,128)(2,1)S(1)} %get-tuple-element.554), channel_id=1, source_target_pairs={{62,0},{63,1},{0,2},{1,3},{2,4},{3,5},{4,6},{5,7},{6,8},{7,9},{8,1... | collective-permute-start | bytes 786440 | tf_op jit(solution)/shard_map/while/body/eval_jaxpr/ppermute | solution.py:18
  108.1 12.6 %collective-permute-start = (bf16[128,2,512]{0,2,1:T(8,128)(2,1)S(1)}, bf16[128,2,512]{0,2,1:T(8,128)(2,1)S(1)}, u32[]{:S(2)}, u32[]{:S(2)}) collective-permute-start(bf16[128,2,512]{0,2,1:T(8,128)(2,1)S(1)} %get-tuple-element.554), channel_id=1, source_target_pairs={{62,0},{63,1},{0,2},{1,3},{2,4},{3,5},{4,6},{5,7},{6,8},{7,9},{8,1... | collective-permute-start | bytes 786440 | tf_op jit(solution)/shard_map/while/body/eval_jaxpr/ppermute | solution.py:18
  121.9 13.8 %collective-permute-start = (bf16[128,2,512]{0,2,1:T(8,128)(2,1)S(1)}, bf16[128,2,512]{0,2,1:T(8,128)(2,1)S(1)}, u32[]{:S(2)}, u32[]{:S(2)}) collective-permute-start(bf16[128,2,512]{0,2,1:T(8,128)(2,1)S(1)} %get-tuple-element.554), channel_id=1, source_target_pairs={{62,0},{63,1},{0,2},{1,3},{2,4},{3,5},{4,6},{5,7},{6,8},{7,9},{8,1... | collective-permute-start | bytes 786440 | tf_op jit(solution)/shard_map/while/body/eval_jaxpr/ppermute | solution.py:18
  136.8 13.9 %collective-permute-start = (bf16[128,2,512]{0,2,1:T(8,128)(2,1)S(1)}, bf16[128,2,512]{0,2,1:T(8,128)(2,1)S(1)}, u32[]{:S(2)}, u32[]{:S(2)}) collective-permute-start(bf16[128,2,512]{0,2,1:T(8,128)(2,1)S(1)} %get-tuple-element.554), channel_id=1, source_target_pairs={{62,0},{63,1},{0,2},{1,3},{2,4},{3,5},{4,6},{5,7},{6,8},{7,9},{8,1... | collective-permute-start | bytes 786440 | tf_op jit(solution)/shard_map/while/body/eval_jaxpr/ppermute | solution.py:18
  151.8 13.1 %collective-permute-start = (bf16[128,2,512]{0,2,1:T(8,128)(2,1)S(1)}, bf16[128,2,512]{0,2,1:T(8,128)(2,1)S(1)}, u32[]{:S(2)}, u32[]{:S(2)}) collective-permute-start(bf16[128,2,512]{0,2,1:T(8,128)(2,1)S(1)} %get-tuple-element.554), channel_id=1, source_target_pairs={{62,0},{63,1},{0,2},{1,3},{2,4},{3,5},{4,6},{5,7},{6,8},{7,9},{8,1... | collective-permute-start | bytes 786440 | tf_op jit(solution)/shard_map/while/body/eval_jaxpr/ppermute | solution.py:18
  166.1 12.2 %collective-permute-start = (bf16[128,2,512]{0,2,1:T(8,128)(2,1)S(1)}, bf16[128,2,512]{0,2,1:T(8,128)(2,1)S(1)}, u32[]{:S(2)}, u32[]{:S(2)}) collective-permute-start(bf16[128,2,512]{0,2,1:T(8,128)(2,1)S(1)} %get-tuple-element.554), channel_id=1, source_target_pairs={{62,0},{63,1},{0,2},{1,3},{2,4},{3,5},{4,6},{5,7},{6,8},{7,9},{8,1... | collective-permute-start | bytes 786440 | tf_op jit(solution)/shard_map/while/body/eval_jaxpr/ppermute | solution.py:18
  179.4 11.6 %collective-permute-start = (bf16[128,2,512]{0,2,1:T(8,128)(2,1)S(1)}, bf16[128,2,512]{0,2,1:T(8,128)(2,1)S(1)}, u32[]{:S(2)}, u32[]{:S(2)}) collective-permute-start(bf16[128,2,512]{0,2,1:T(8,128)(2,1)S(1)} %get-tuple-element.554), channel_id=1, source_target_pairs={{62,0},{63,1},{0,2},{1,3},{2,4},{3,5},{4,6},{5,7},{6,8},{7,9},{8,1... | collective-permute-start | bytes 786440 | tf_op jit(solution)/shard_map/while/body/eval_jaxpr/ppermute | solution.py:18
  192.2 11.6 %collective-permute-start = (bf16[128,2,512]{0,2,1:T(8,128)(2,1)S(1)}, bf16[128,2,512]{0,2,1:T(8,128)(2,1)S(1)}, u32[]{:S(2)}, u32[]{:S(2)}) collective-permute-start(bf16[128,2,512]{0,2,1:T(8,128)(2,1)S(1)} %get-tuple-element.554), channel_id=1, source_target_pairs={{62,0},{63,1},{0,2},{1,3},{2,4},{3,5},{4,6},{5,7},{6,8},{7,9},{8,1... | collective-permute-start | bytes 786440 | tf_op jit(solution)/shard_map/while/body/eval_jaxpr/ppermute | solution.py:18
  204.9 11.6 %collective-permute-start = (bf16[128,2,512]{0,2,1:T(8,128)(2,1)S(1)}, bf16[128,2,512]{0,2,1:T(8,128)(2,1)S(1)}, u32[]{:S(2)}, u32[]{:S(2)}) collective-permute-start(bf16[128,2,512]{0,2,1:T(8,128)(2,1)S(1)} %get-tuple-element.554), channel_id=1, source_target_pairs={{62,0},{63,1},{0,2},{1,3},{2,4},{3,5},{4,6},{5,7},{6,8},{7,9},{8,1... | collective-permute-start | bytes 786440 | tf_op jit(solution)/shard_map/while/body/eval_jaxpr/ppermute | solution.py:18
  217.6 11.6 %collective-permute-start = (bf16[128,2,512]{0,2,1:T(8,128)(2,1)S(1)}, bf16[128,2,512]{0,2,1:T(8,128)(2,1)S(1)}, u32[]{:S(2)}, u32[]{:S(2)}) collective-permute-start(bf16[128,2,512]{0,2,1:T(8,128)(2,1)S(1)} %get-tuple-element.554), channel_id=1, source_target_pairs={{62,0},{63,1},{0,2},{1,3},{2,4},{3,5},{4,6},{5,7},{6,8},{7,9},{8,1... | collective-permute-start | bytes 786440 | tf_op jit(solution)/shard_map/while/body/eval_jaxpr/ppermute | solution.py:18
  230.4 11.6 %collective-permute-start = (bf16[128,2,512]{0,2,1:T(8,128)(2,1)S(1)}, bf16[128,2,512]{0,2,1:T(8,128)(2,1)S(1)}, u32[]{:S(2)}, u32[]{:S(2)}) collective-permute-start(bf16[128,2,512]{0,2,1:T(8,128)(2,1)S(1)} %get-tuple-element.554), channel_id=1, source_target_pairs={{62,0},{63,1},{0,2},{1,3},{2,4},{3,5},{4,6},{5,7},{6,8},{7,9},{8,1... | collective-permute-start | bytes 786440 | tf_op jit(solution)/shard_map/while/body/eval_jaxpr/ppermute | solution.py:18
  243.1 11.6 %collective-permute-start = (bf16[128,2,512]{0,2,1:T(8,128)(2,1)S(1)}, bf16[128,2,512]{0,2,1:T(8,128)(2,1)S(1)}, u32[]{:S(2)}, u32[]{:S(2)}) collective-permute-start(bf16[128,2,512]{0,2,1:T(8,128)(2,1)S(1)} %get-tuple-element.554), channel_id=1, source_target_pairs={{62,0},{63,1},{0,2},{1,3},{2,4},{3,5},{4,6},{5,7},{6,8},{7,9},{8,1... | collective-permute-start | bytes 786440 | tf_op jit(solution)/shard_map/while/body/eval_jaxpr/ppermute | solution.py:18
  255.9 12.7 %collective-permute-start = (bf16[128,2,512]{0,2,1:T(8,128)(2,1)S(1)}, bf16[128,2,512]{0,2,1:T(8,128)(2,1)S(1)}, u32[]{:S(2)}, u32[]{:S(2)}) collective-permute-start(bf16[128,2,512]{0,2,1:T(8,128)(2,1)S(1)} %get-tuple-element.554), channel_id=1, source_target_pairs={{62,0},{63,1},{0,2},{1,3},{2,4},{3,5},{4,6},{5,7},{6,8},{7,9},{8,1... | collective-permute-start | bytes 786440 | tf_op jit(solution)/shard_map/while/body/eval_jaxpr/ppermute | solution.py:18
  269.8 13.9 %collective-permute-start = (bf16[128,2,512]{0,2,1:T(8,128)(2,1)S(1)}, bf16[128,2,512]{0,2,1:T(8,128)(2,1)S(1)}, u32[]{:S(2)}, u32[]{:S(2)}) collective-permute-start(bf16[128,2,512]{0,2,1:T(8,128)(2,1)S(1)} %get-tuple-element.554), channel_id=1, source_target_pairs={{62,0},{63,1},{0,2},{1,3},{2,4},{3,5},{4,6},{5,7},{6,8},{7,9},{8,1... | collective-permute-start | bytes 786440 | tf_op jit(solution)/shard_map/while/body/eval_jaxpr/ppermute | solution.py:18
  284.9 13.7 %collective-permute-start = (bf16[128,2,512]{0,2,1:T(8,128)(2,1)S(1)}, bf16[128,2,512]{0,2,1:T(8,128)(2,1)S(1)}, u32[]{:S(2)}, u32[]{:S(2)}) collective-permute-start(bf16[128,2,512]{0,2,1:T(8,128)(2,1)S(1)} %get-tuple-element.554), channel_id=1, source_target_pairs={{62,0},{63,1},{0,2},{1,3},{2,4},{3,5},{4,6},{5,7},{6,8},{7,9},{8,1... | collective-permute-start | bytes 786440 | tf_op jit(solution)/shard_map/while/body/eval_jaxpr/ppermute | solution.py:18
  299.7 12.9 %collective-permute-start = (bf16[128,2,512]{0,2,1:T(8,128)(2,1)S(1)}, bf16[128,2,512]{0,2,1:T(8,128)(2,1)S(1)}, u32[]{:S(2)}, u32[]{:S(2)}) collective-permute-start(bf16[128,2,512]{0,2,1:T(8,128)(2,1)S(1)} %get-tuple-element.554), channel_id=1, source_target_pairs={{62,0},{63,1},{0,2},{1,3},{2,4},{3,5},{4,6},{5,7},{6,8},{7,9},{8,1... | collective-permute-start | bytes 786440 | tf_op jit(solution)/shard_map/while/body/eval_jaxpr/ppermute | solution.py:18
  313.8 12.0 %collective-permute-start = (bf16[128,2,512]{0,2,1:T(8,128)(2,1)S(1)}, bf16[128,2,512]{0,2,1:T(8,128)(2,1)S(1)}, u32[]{:S(2)}, u32[]{:S(2)}) collective-permute-start(bf16[128,2,512]{0,2,1:T(8,128)(2,1)S(1)} %get-tuple-element.554), channel_id=1, source_target_pairs={{62,0},{63,1},{0,2},{1,3},{2,4},{3,5},{4,6},{5,7},{6,8},{7,9},{8,1... | collective-permute-start | bytes 786440 | tf_op jit(solution)/shard_map/while/body/eval_jaxpr/ppermute | solution.py:18
  326.9 11.6 %collective-permute-start = (bf16[128,2,512]{0,2,1:T(8,128)(2,1)S(1)}, bf16[128,2,512]{0,2,1:T(8,128)(2,1)S(1)}, u32[]{:S(2)}, u32[]{:S(2)}) collective-permute-start(bf16[128,2,512]{0,2,1:T(8,128)(2,1)S(1)} %get-tuple-element.554), channel_id=1, source_target_pairs={{62,0},{63,1},{0,2},{1,3},{2,4},{3,5},{4,6},{5,7},{6,8},{7,9},{8,1... | collective-permute-start | bytes 786440 | tf_op jit(solution)/shard_map/while/body/eval_jaxpr/ppermute | solution.py:18
  339.7 11.6 %collective-permute-start = (bf16[128,2,512]{0,2,1:T(8,128)(2,1)S(1)}, bf16[128,2,512]{0,2,1:T(8,128)(2,1)S(1)}, u32[]{:S(2)}, u32[]{:S(2)}) collective-permute-start(bf16[128,2,512]{0,2,1:T(8,128)(2,1)S(1)} %get-tuple-element.554), channel_id=1, source_target_pairs={{62,0},{63,1},{0,2},{1,3},{2,4},{3,5},{4,6},{5,7},{6,8},{7,9},{8,1... | collective-permute-start | bytes 786440 | tf_op jit(solution)/shard_map/while/body/eval_jaxpr/ppermute | solution.py:18
  352.4 11.6 %collective-permute-start = (bf16[128,2,512]{0,2,1:T(8,128)(2,1)S(1)}, bf16[128,2,512]{0,2,1:T(8,128)(2,1)S(1)}, u32[]{:S(2)}, u32[]{:S(2)}) collective-permute-start(bf16[128,2,512]{0,2,1:T(8,128)(2,1)S(1)} %get-tuple-element.554), channel_id=1, source_target_pairs={{62,0},{63,1},{0,2},{1,3},{2,4},{3,5},{4,6},{5,7},{6,8},{7,9},{8,1... | collective-permute-start | bytes 786440 | tf_op jit(solution)/shard_map/while/body/eval_jaxpr/ppermute | solution.py:18
  365.1 11.6 %collective-permute-start = (bf16[128,2,512]{0,2,1:T(8,128)(2,1)S(1)}, bf16[128,2,512]{0,2,1:T(8,128)(2,1)S(1)}, u32[]{:S(2)}, u32[]{:S(2)}) collective-permute-start(bf16[128,2,512]{0,2,1:T(8,128)(2,1)S(1)} %get-tuple-element.554), channel_id=1, source_target_pairs={{62,0},{63,1},{0,2},{1,3},{2,4},{3,5},{4,6},{5,7},{6,8},{7,9},{8,1... | collective-permute-start | bytes 786440 | tf_op jit(solution)/shard_map/while/body/eval_jaxpr/ppermute | solution.py:18
  377.9 11.6 %collective-permute-start = (bf16[128,2,512]{0,2,1:T(8,128)(2,1)S(1)}, bf16[128,2,512]{0,2,1:T(8,128)(2,1)S(1)}, u32[]{:S(2)}, u32[]{:S(2)}) collective-permute-start(bf16[128,2,512]{0,2,1:T(8,128)(2,1)S(1)} %get-tuple-element.554), channel_id=1, source_target_pairs={{62,0},{63,1},{0,2},{1,3},{2,4},{3,5},{4,6},{5,7},{6,8},{7,9},{8,1... | collective-permute-start | bytes 786440 | tf_op jit(solution)/shard_map/while/body/eval_jaxpr/ppermute | solution.py:18
  390.6 11.6 %collective-permute-start = (bf16[128,2,512]{0,2,1:T(8,128)(2,1)S(1)}, bf16[128,2,512]{0,2,1:T(8,128)(2,1)S(1)}, u32[]{:S(2)}, u32[]{:S(2)}) collective-permute-start(bf16[128,2,512]{0,2,1:T(8,128)(2,1)S(1)} %get-tuple-element.554), channel_id=1, source_target_pairs={{62,0},{63,1},{0,2},{1,3},{2,4},{3,5},{4,6},{5,7},{6,8},{7,9},{8,1... | collective-permute-start | bytes 786440 | tf_op jit(solution)/shard_map/while/body/eval_jaxpr/ppermute | solution.py:18
  403.4 11.6 %collective-permute-start = (bf16[128,2,512]{0,2,1:T(8,128)(2,1)S(1)}, bf16[128,2,512]{0,2,1:T(8,128)(2,1)S(1)}, u32[]{:S(2)}, u32[]{:S(2)}) collective-permute-start(bf16[128,2,512]{0,2,1:T(8,128)(2,1)S(1)} %get-tuple-element.554), channel_id=1, source_target_pairs={{62,0},{63,1},{0,2},{1,3},{2,4},{3,5},{4,6},{5,7},{6,8},{7,9},{8,1... | collective-permute-start | bytes 786440 | tf_op jit(solution)/shard_map/while/body/eval_jaxpr/ppermute | solution.py:18
  416.5 16.7 %collective-permute-start.1 = (bf16[1,128,1536]{1,2,0:T(8,128)(2,1)S(1)}, bf16[1,128,1536]{1,2,0:T(8,128)(2,1)S(1)}, u32[]{:S(2)}, u32[]{:S(2)}) collective-permute-start(bf16[1,128,1536]{1,2,0:T(8,128)(2,1)S(1)} %bitcast.57), channel_id=1, source_target_pairs={{448,0},{0,64},{64,128},{128,192},{192,256},{256,320},{320,384},{3... | collective-permute-start | bytes 1179656 | tf_op jit(solution)/shard_map/ppermute | solution.py:18
where the time goes:
time: 436 us; the launch traced here: 434 us
  waiting for transfers between devices  321 us (74%)
  starting transfers between devices  65.3 us (15%)
  matrix products  28.7 us (7%)
  other arithmetic  10.4 us (2%)
  local copies, waits for them, and re-layouts  5.02 us (1%)
    ppermute x32, waiting for transfers between devices, passed_along(): return lax.ppermute(block, axis, route)  321 us
    ppermute x32, starting transfers between devices, passed_along(): return lax.ppermute(block, axis, route)  65.3 us
    dot_general x32, matrix products, attend(): jnp.einsum('hgqk,khd->hgqd', weights.astype(jnp.bfloat16), values, prefer...  17.4 us
    dot_general x32, matrix products, attend(): jnp.einsum('qhgd,khd->hgqk', q_rows, keys, preferred_element_type=jnp.flo...  11.3 us
  transfers between devices with their start and end apart: 32, of which 32 were waited for; matrix products, arithmetic and copies ran while one was open for 1% of the time, Pallas kernels for 0%

commit v1 on v0

v1 whole, which is shorter than its diff:
```python
import functools
import math

import jax
import jax.numpy as jnp
from jax import lax
from jax.experimental import pallas as pl
from jax.experimental.pallas import tpu as pltpu
from jax.sharding import PartitionSpec as P

HD = 128
KVH = 4
SHARE = 3
NSEQ = 2
NX = 4
NY = 8
HALF = 64
BLK = NX * HALF
NEG = -1e30
MESH = pl.DeviceIdType.MESH
A, B = 0, 1


def kernel(q_ref, kv_ref, out_ref, kvs, kvbuf, qbuf, obuf, top, total, acc,
           kv_send, kv_recv, q_send, q_recv, q_own, up_send, up_recv, down_send, down_recv,
           out_send, out_recv):
    pipe = lax.axis_index("pipe")
    ctx = lax.axis_index("ctx")
    core = lax.rem(ctx, NSEQ)
    x = lax.rem(ctx // NSEQ, NX)
    y = ctx // (NSEQ * NX)
    npipe = lax.axis_size("pipe")
    nxt, prv = lax.rem(pipe + 1, npipe), lax.rem(pipe + npipe - 1, npipe)

    def at(px, py):
        return (py * NX + px) * NSEQ + core

    up = (pipe, at(x, lax.rem(y + 1, NY)))
    down = (pipe, at(x, lax.rem(y + NY - 1, NY)))
    peers = [(lax.rem(x + j, NX), lax.rem(x + NX - j, NX)) for j in range(NX)]

    barrier = pltpu.get_barrier_semaphore()

    def greet(device):
        pl.semaphore_signal(barrier, inc=1, device_id=device, device_id_type=MESH)

    for j in range(1, NX):
        greet((pipe, at(peers[j][0], y)))
    greet(up)
    greet(down)
    for j in range(NX):
        greet((prv, at(peers[j][0], y)))

    for i in range(2):
        for part in range(2):
            rows = kv_ref[0, part * HALF:(part + 1) * HALF, i, :]
            for h in range(KVH):
                kvs[h, part, i] = rows[:, h * HD:(h + 1) * HD]

    pl.semaphore_wait(barrier, 2 * NX + 1)

    def place(px, part):
        return (px if part == A else NX - 1 - px) * HALF

    def kv_copy(j, part):
        to, _ = peers[j]
        return pltpu.make_async_remote_copy(
            src_ref=kvs.at[to, part],
            dst_ref=kvbuf.at[y, part, :, pl.ds(pl.multiple_of(place(x, part), HALF), HALF), :],
            send_sem=kv_send.at[j, part], recv_sem=kv_recv.at[j, part],
            device_id=(pipe, at(to, y)), device_id_type=MESH)

    def q_copy(j, part):
        to, _ = peers[j]
        return pltpu.make_async_remote_copy(
            src_ref=q_ref.at[0, pl.ds(part * HALF, HALF), pl.ds(pl.multiple_of(to * SHARE * HD, HD), SHARE * HD)],
            dst_ref=qbuf.at[part, pl.ds(pl.multiple_of(place(x, part), HALF), HALF), :],
            send_sem=q_send.at[j, part], recv_sem=q_recv.at[j, part],
            device_id=(pipe, at(to, y)), device_id_type=MESH)

    def q_local(part):
        return pltpu.make_async_copy(
            q_ref.at[0, pl.ds(part * HALF, HALF), pl.ds(pl.multiple_of(x * SHARE * HD, HD), SHARE * HD)],
            qbuf.at[part, pl.ds(pl.multiple_of(place(x, part), HALF), HALF), :],
            q_own.at[part])

    for part in (A, B):
        for j in (1, 3, 2):
            kv_copy(j, part).start()
    for part in (A, B):
        q_local(part).start()
        for j in (1, 3, 2):
            q_copy(j, part).start()
    for part in (A, B):
        kvbuf[y, part, :, pl.ds(pl.multiple_of(place(x, part), HALF), HALF), :] = kvs[x, part]

    top[...] = jnp.full_like(top, NEG)
    total[...] = jnp.zeros_like(total)
    acc[...] = jnp.zeros_like(acc)

    def ring(upward, part, d):
        owner = lax.rem(y + NY - d, NY) if upward else lax.rem(y + d, NY)
        slot = kvbuf.at[owner, part]
        send, recv = (up_send, up_recv) if upward else (down_send, down_recv)
        return pltpu.make_async_remote_copy(
            src_ref=slot, dst_ref=slot, send_sem=send.at[part, d], recv_sem=recv.at[part, d],
            device_id=up if upward else down, device_id_type=MESH)

    def arrived(upward, part, d):
        owner = lax.rem(y + NY - d, NY) if upward else lax.rem(y + d, NY)
        slot = kvbuf.at[owner, part]
        send, recv = (up_send, up_recv) if upward else (down_send, down_recv)
        pltpu.make_async_remote_copy(
            src_ref=slot, dst_ref=slot, send_sem=send.at[part, d - 1], recv_sem=recv.at[part, d - 1],
            device_id=up if upward else down, device_id_type=MESH).wait_recv()
        return owner

    for part in (A, B):
        for j in (1, 3, 2):
            kv_copy(j, part).wait_recv()
        ring(True, part, 0).start()
        ring(False, part, 0).start()
    for part in (A, B):
        q_local(part).wait()
        for j in (1, 3, 2):
            q_copy(j, part).wait_recv()

    factor = math.log2(math.e) / math.sqrt(HD)

    def attend(rows, owner, part, masked):
        keys, values = kvbuf[owner, part, 0], kvbuf[owner, part, 1]
        for g in range(SHARE):
            q = qbuf[rows, :, g * HD:(g + 1) * HD]
            s = lax.dot_general(keys, q, (((1,), (1,)), ((), ())), preferred_element_type=jnp.float32)
            if masked:
                k_at = lax.broadcasted_iota(jnp.int32, (BLK, BLK), 0)
                q_at = lax.broadcasted_iota(jnp.int32, (BLK, BLK), 1)
                s = jnp.where(k_at <= q_at, s, NEG)
            old = top[rows, g]
            new = jnp.maximum(old, jnp.max(s, axis=0, keepdims=True))
            fade = jnp.exp2((old - new) * factor)
            w = jnp.exp2((s - new) * factor)
            top[rows, g] = new
            total[rows, g] = total[rows, g] * fade + jnp.sum(w, axis=0, keepdims=True)
            acc[rows, g] = acc[rows, g] * fade + lax.dot_general(
                values, w.astype(jnp.bfloat16), (((0,), (0,)), ((), ())), preferred_element_type=jnp.float32)

    def diagonal(rows, _):
        attend(rows, y, rows, True)
        return 0

    lax.fori_loop(0, 2, diagonal, 0)
    attend(B, y, A, False)

    def span(lo, hi, owner, part):
        def one(rows, _):
            attend(rows, owner, part, False)
            return 0
        lax.fori_loop(lo, hi, one, 0)

    def use(owner, part):
        if part == A:
            span(jnp.where(owner < y, 0, 1), 2, owner, A)
        else:
            span(1, jnp.where(owner > y, 2, 1), owner, B)

    def step(d, _):
        for part in (A, B):
            for upward in (True, False):
                owner = arrived(upward, part, d)
                last = 4 if upward == (part == A) else 3

                @pl.when(d < last)
                def _():
                    ring(upward, part, d).start()

                use(owner, part)
        return 0

    lax.fori_loop(1, 4, step, 0)
    use(arrived(True, A, 4), A)
    use(arrived(False, B, 4), B)

    def out_copy(j, part):
        to, _ = peers[j]
        return pltpu.make_async_remote_copy(
            src_ref=obuf.at[part, pl.ds(pl.multiple_of(place(to, part), HALF), HALF), :],
            dst_ref=out_ref.at[0, pl.ds(part * HALF, HALF), pl.ds(pl.multiple_of(x * SHARE * HD, HD), SHARE * HD)],
            send_sem=out_send.at[j, part], recv_sem=out_recv.at[j, part],
            device_id=(nxt, at(to, y)), device_id_type=MESH)

    def out_wait(j, part):
        _, frm = peers[j]
        pltpu.make_async_remote_copy(
            src_ref=obuf.at[part, pl.ds(0, HALF), :],
            dst_ref=out_ref.at[0, pl.ds(part * HALF, HALF), pl.ds(pl.multiple_of(frm * SHARE * HD, HD), SHARE * HD)],
            send_sem=out_send.at[j, part], recv_sem=out_recv.at[j, part],
            device_id=(nxt, at(frm, y)), device_id_type=MESH).wait_recv()

    for part in (A, B):
        for g in range(SHARE):
            o = acc[part, g] / total[part, g]
            obuf[part, :, g * HD:(g + 1) * HD] = o.T.astype(jnp.bfloat16)
        for j in (2, 1, 3, 0):
            out_copy(j, part).start()

    for part in (A, B):
        for j in range(1, NX):
            kv_copy(j, part).wait_send()
            q_copy(j, part).wait_send()
        for d in range(4):
            for upward in (True, False):
                if d < (4 if upward == (part == A) else 3):
                    ring(upward, part, d).wait_send()
        for j in range(NX):
            out_copy(j, part).wait_send()
            out_wait(j, part)


def shards(queries, keys_values):
    dma = pltpu.SemaphoreType.DMA
    return pl.pallas_call(
        kernel,
        out_shape=jax.ShapeDtypeStruct(queries.shape, jnp.bfloat16),
        in_specs=[pl.BlockSpec(memory_space=pl.ANY), pl.BlockSpec(memory_space=pltpu.VMEM)],
        out_specs=pl.BlockSpec(memory_space=pl.ANY),
        scratch_shapes=[
            pltpu.VMEM((KVH, 2, 2, HALF, HD), jnp.bfloat16),
            pltpu.VMEM((NY, 2, 2, BLK, HD), jnp.bfloat16),
            pltpu.VMEM((2, BLK, SHARE * HD), jnp.bfloat16),
            pltpu.VMEM((2, BLK, SHARE * HD), jnp.bfloat16),
            pltpu.VMEM((2, SHARE, 1, BLK), jnp.float32),
            pltpu.VMEM((2, SHARE, 1, BLK), jnp.float32),
            pltpu.VMEM((2, SHARE, HD, BLK), jnp.float32),
            dma((NX, 2)), dma((NX, 2)), dma((NX, 2)), dma((NX, 2)), dma((2,)),
            dma((2, 4)), dma((2, 4)), dma((2, 4)), dma((2, 4)),
            dma((NX, 2)), dma((NX, 2)),
        ],
        compiler_params=pltpu.CompilerParams(
            collective_id=0, has_side_effects=True, vmem_limit_bytes=48 * 1024 * 1024),
        cost_estimate=pl.CostEstimate(flops=3_500_000_000, bytes_accessed=4_000_000, transcendentals=3_400_000),
    )(queries, keys_values)


def solution(mesh):
    placed = (P("pipe", "ctx", None), P("pipe", "ctx", None, None))
    return jax.shard_map(
        shards, mesh=mesh, in_specs=placed, out_specs=P("pipe", "ctx", None), check_vma=False
    )
```

time: 436 us -> 57.1 us (0.13)
  the two profiles are of different devices: /device:TPU:32 before, /device:TPU:16 now
where the time goes in v1:
time: 57.1 us; the launch traced here: 57 us
  Pallas kernels  54.2 us (95%)
  local copies, waits for them, and re-layouts  2.69 us (5%)
    pallas_call x1, Pallas kernels, shards(): pl.pallas_call(kernel, out_shape=jax.ShapeDtypeStruct(queries.shape, jnp....  54.2 us
    unnamed x5, local copies, waits for them, and re-layouts  2.69 us

profile of v1, /device:TPU:16, one launch (start us, length us, event | category | flops | bytes accessed | tf_op | source)
XLA Modules:
  0.0 57.0 jit_solution(8071621910640750616)
XLA Ops:
  0.0 0.0 copy-start
  0.0 1.0 %copy-done = bf16[1,128,1536]{2,1,0:T(8,128)(2,1)S(1)} copy-done((bf16[1,128,1536]{2,1,0:T(8,128)(2,1)S(1)}, bf16[1,128,1536]{2,1,0:T(8,128)(2,1)}, u32[]{:S(2)}) %copy-start) | copy-done | bytes 393240
  1.0 0.0 copy-start.1
  1.0 0.9 %copy-done.1 = bf16[1,128,2,512]{3,2,1,0:T(2,128)(2,1)S(1)} copy-done((bf16[1,128,2,512]{3,2,1,0:T(2,128)(2,1)S(1)}, bf16[1,128,2,512]{3,2,1,0:T(2,128)(2,1)}, u32[]{:S(2)}) %copy-start.1) | copy-done | bytes 262168
  1.9 54.2 %shard_map.28 = bf16[1,128,1536]{2,1,0:T(8,128)(2,1)S(1)} custom-call(bf16[1,128,1536]{2,1,0:T(8,128)(2,1)S(1)} %copy-done, bf16[1,128,2,512]{3,2,1,0:T(2,128)(2,1)S(1)} %copy-done.1), custom_call_target="tpu_custom_call" | custom-call | flops 3500000000 | bytes 4000000 | tf_op jit(solution)/shard_map/pallas_call | solution.py:222
  56.2 0.7 %copy.4 = bf16[1,128,1536]{2,1,0:T(8,128)(2,1)} copy(bf16[1,128,1536]{2,1,0:T(8,128)(2,1)S(1)} %shard_map.28) | data formatting | bytes 786432
Async XLA Ops:
  0.0 1.0 %copy-start = (bf16[1,128,1536]{2,1,0:T(8,128)(2,1)S(1)}, bf16[1,128,1536]{2,1,0:T(8,128)(2,1)}, u32[]{:S(2)}) copy-start(bf16[1,128,1536]{2,1,0:T(8,128)(2,1)} %q_ref.1) | copy-start | bytes 1179652
  1.0 0.9 %copy-start.1 = (bf16[1,128,2,512]{3,2,1,0:T(2,128)(2,1)S(1)}, bf16[1,128,2,512]{3,2,1,0:T(2,128)(2,1)}, u32[]{:S(2)}) copy-start(bf16[1,128,2,512]{3,2,1,0:T(2,128)(2,1)} %kv_ref.1) | copy-start | bytes 786436

commit v2 on v0

v2 whole, which is shorter than its diff:
```python
import functools
import math

import jax
import jax.numpy as jnp
from jax import lax
from jax.experimental import pallas as pl
from jax.experimental.pallas import tpu as pltpu
from jax.sharding import PartitionSpec as P

HD = 128
KVH = 4
SHARE = 3
NSEQ = 2
NX = 4
NY = 8
FAR = NY // 2
HALF = 64
BLK = NX * HALF
ROWS = SHARE * BLK
WIDE = SHARE * HD
GO = 2
NEG = -1e30
MESH = pl.DeviceIdType.MESH
A, B = 0, 1


def kernel(q_ref, kv_ref, out_ref, kvin, kvs, kvbuf, qbuf, qs, obuf, top, total, acc,
           load, kv_send, kv_recv, q_send, q_recv, up_send, up_recv, down_send, down_recv,
           out_send, out_recv, go):
    pipe = lax.axis_index("pipe")
    ctx = lax.axis_index("ctx")
    core = lax.rem(ctx, NSEQ)
    x = lax.rem(ctx // NSEQ, NX)
    y = ctx // (NSEQ * NX)
    npipe = lax.axis_size("pipe")
    nxt, prv = lax.rem(pipe + 1, npipe), lax.rem(pipe + npipe - 1, npipe)
    first = core == 1
    in_pipe = jnp.where(first, pipe, nxt)
    out_pipe = jnp.where(first, nxt, pipe)

    def at(px, py):
        return (py * NX + px) * NSEQ + core

    up = (pipe, at(x, lax.rem(y + 1, NY)))
    down = (pipe, at(x, lax.rem(y + NY - 1, NY)))
    twin = (pipe, (y * NX + x) * NSEQ + 1 - core)
    peers = [(lax.rem(x + j, NX), lax.rem(x + NX - j, NX)) for j in range(NX)]

    kv_in = pltpu.make_async_copy(kv_ref.at[0], kvin, load)
    kv_in.start()

    barrier = pltpu.get_barrier_semaphore()

    def greet(device):
        pl.semaphore_signal(barrier, inc=1, device_id=device, device_id_type=MESH)

    for j in range(1, NX):
        greet((pipe, at(peers[j][0], y)))
    greet(up)
    greet(down)
    greet(twin)
    for j in range(NX):
        greet((prv, at(peers[j][0], y)))

    kv_in.wait()
    for i in range(2):
        for part in range(2):
            rows = kvin[part * HALF:(part + 1) * HALF, i, :]
            for h in range(KVH):
                kvs[h, part, i] = rows[:, h * HD:(h + 1) * HD]

    pl.semaphore_wait(barrier, 2 * NX + 2)

    def place(px, part):
        return pl.ds(pl.multiple_of((px if part == A else NX - 1 - px) * HALF, HALF), HALF)

    def head(h):
        return pl.ds(pl.multiple_of(h * WIDE, HD), WIDE)

    def kv_ends(j, part):
        return kvs.at[peers[j][0], part], kvbuf.at[y, part, :, place(x, part), :]

    def q_ends(j, part):
        return q_ref.at[0, pl.ds(part * HALF, HALF), head(peers[j][0])], qbuf.at[part, place(x, part), :]

    def out_ends(j, part):
        return obuf.at[part, place(peers[j][0], part), :], out_ref.at[0, pl.ds(part * HALF, HALF), head(x)]

    def remote(ends, send, recv, j, part, to_pipe):
        src, dst = ends(j, part)
        return pltpu.make_async_remote_copy(
            src_ref=src, dst_ref=dst, send_sem=send.at[j, part], recv_sem=recv.at[j, part],
            device_id=(to_pipe, at(peers[j][0], y)), device_id_type=MESH)

    def local(ends, recv, part):
        src, dst = ends(0, part)
        return pltpu.make_async_copy(src, dst, recv.at[0, part])

    kv_copy = lambda j, part: remote(kv_ends, kv_send, kv_recv, j, part, in_pipe)
    q_copy = lambda j, part: remote(q_ends, q_send, q_recv, j, part, in_pipe)
    out_copy = lambda j, part: remote(out_ends, out_send, out_recv, j, part, out_pipe)

    def begin(copy, ends, recv, part, stays):
        @pl.when(stays)
        def _():
            local(ends, recv, part).start()

        @pl.when(jnp.logical_not(stays))
        def _():
            copy(0, part).start()

        for j in (1, 3, 2):
            copy(j, part).start()

    def landed(copy, ends, recv, j, part, stays):
        if j > 0:
            copy(j, part).wait_recv()
            return

        @pl.when(stays)
        def _():
            local(ends, recv, part).wait()

        @pl.when(jnp.logical_not(stays))
        def _():
            copy(0, part).wait_recv()

    def sent(copy, part, stays):
        @pl.when(jnp.logical_not(stays))
        def _():
            copy(0, part).wait_send()

        for j in (1, 3, 2):
            copy(j, part).wait_send()

    begin(kv_copy, kv_ends, kv_recv, A, first)
    begin(kv_copy, kv_ends, kv_recv, B, first)
    begin(q_copy, q_ends, q_recv, A, first)
    begin(q_copy, q_ends, q_recv, B, first)

    top[...] = jnp.full_like(top, NEG)
    total[...] = jnp.zeros_like(total)
    acc[...] = jnp.zeros_like(acc)

    def owner_of(upward, d):
        return lax.rem(y + NY - d, NY) if upward else lax.rem(y + d, NY)

    def ring(upward, part, d):
        slot = kvbuf.at[owner_of(upward, d), part]
        send, recv = (up_send, up_recv) if upward else (down_send, down_recv)
        return pltpu.make_async_remote_copy(
            src_ref=slot, dst_ref=slot, send_sem=send.at[part, d], recv_sem=recv.at[part, d],
            device_id=up if upward else down, device_id_type=MESH)

    def needed(upward, part, d):
        hops = FAR if upward == (part == A) else FAR - 1
        ok = d < hops
        if part == B:
            owner = owner_of(upward, d)
            ok = jnp.logical_and(ok, owner + FAR - 1 >= NY if upward else owner - d - 1 >= 0)
        return ok

    def pass_on(upward, part, d):
        @pl.when(needed(upward, part, d))
        def _():
            ring(upward, part, d).start()

    def arrive(upward, part, d):
        owner = owner_of(upward, d)
        ok = True if part == A else (owner + FAR - 1 >= NY if upward else y + d < NY)
        slot = kvbuf.at[owner, part]
        send, recv = (up_send, up_recv) if upward else (down_send, down_recv)

        @pl.when(ok)
        def _():
            pltpu.make_async_remote_copy(
                src_ref=slot, dst_ref=slot, send_sem=send.at[part, d - 1], recv_sem=recv.at[part, d - 1],
                device_id=up if upward else down, device_id_type=MESH).wait_recv()

        pass_on(upward, part, d)

    last_plane = pipe == npipe - 1

    @pl.when(jnp.logical_and(last_plane, jnp.logical_not(first)))
    def _():
        pl.semaphore_wait(go, 1)

    for part, j in ((A, 0), (B, 0), (A, 1), (A, 3), (A, 2), (B, 1), (B, 3), (B, 2)):
        landed(kv_copy, kv_ends, kv_recv, j, part, first)
        piece = kvbuf.at[y, part, :, place(peers[j][1], part), :]
        for upward in (True, False):
            @pl.when(needed(upward, part, 0))
            def _():
                pltpu.make_async_remote_copy(
                    src_ref=piece, dst_ref=piece,
                    send_sem=(up_send if upward else down_send).at[part, 0],
                    recv_sem=(up_recv if upward else down_recv).at[part, 0],
                    device_id=up if upward else down, device_id_type=MESH).start()

    for part in (A, B):
        for j in range(NX):
            landed(q_copy, q_ends, q_recv, j, part, first)
        for g in range(SHARE):
            qs[part, g * BLK:(g + 1) * BLK, :] = qbuf[part, :, g * HD:(g + 1) * HD]

    factor = math.log2(math.e) / math.sqrt(HD)

    def attend(rows, blocks, shift=None):
        keys = jnp.concatenate([kvbuf[o, p, 0] for o, p in blocks], axis=0)
        values = jnp.concatenate([kvbuf[o, p, 1] for o, p in blocks], axis=0)
        count = len(blocks) * BLK
        s = lax.dot_general(qs[rows], keys, (((1,), (1,)), ((), ())), preferred_element_type=jnp.float32)
        if shift is not None:
            q_at = lax.broadcasted_iota(jnp.int32, (SHARE, BLK, count), 1).reshape(ROWS, count)
            k_at = lax.broadcasted_iota(jnp.int32, (ROWS, count), 1)
            s = jnp.where(k_at <= q_at + shift, s, NEG)
        old = top[rows]
        new = jnp.maximum(old, jnp.max(s, axis=1, keepdims=True))
        fade = jnp.exp2((old - new) * factor)
        w = jnp.exp2((s - jnp.concatenate([new] * (count // HD), axis=1)) * factor)
        top[rows] = new
        total[rows] = total[rows] * fade + jnp.sum(w, axis=1, keepdims=True)
        acc[rows] = acc[rows] * fade + jnp.dot(w.astype(jnp.bfloat16), values, preferred_element_type=jnp.float32)

    attend(A, [(y, A)], 0)
    attend(B, [(y, A), (y, B)], BLK)

    def same(d):
        for upward in (True, False):
            owner = owner_of(upward, d)
            part = jnp.where(owner < y, A, B)
            attend(part, [(owner, part)])

    def step(d, _):
        arrive(True, A, d)
        arrive(False, A, d)

        @pl.when(d > 1)
        def _():
            same(d - 1)

        arrive(True, B, d)
        arrive(False, B, d)

        @pl.when(jnp.logical_and(d == GO, jnp.logical_and(last_plane, first)))
        def _():
            pl.semaphore_signal(go, inc=1, device_id=twin, device_id_type=MESH)

        attend(B, [(owner_of(True, d), A), (owner_of(False, d), A)])
        return 0

    lax.fori_loop(1, FAR, step, 0)
    same(FAR - 1)
    arrive(True, A, FAR)
    far = owner_of(True, FAR)

    @pl.when(far < y)
    def _():
        attend(A, [(far, A)])

    def finish(part):
        o = acc[part] / total[part]
        for g in range(SHARE):
            obuf[part, :, g * HD:(g + 1) * HD] = o[g * BLK:(g + 1) * BLK].astype(jnp.bfloat16)
        begin(out_copy, out_ends, out_recv, part, jnp.logical_not(first))

    finish(A)
    arrive(False, B, FAR)

    @pl.when(far < y)
    def _():
        attend(B, [(far, A)])

    @pl.when(far > y)
    def _():
        attend(B, [(far, A), (far, B)])

    finish(B)

    for part in (A, B):
        sent(kv_copy, part, first)
        sent(q_copy, part, first)
        for d in range(FAR):
            for upward in (True, False):
                @pl.when(needed(upward, part, d))
                def _():
                    ring(upward, part, d).wait_send()
        sent(out_copy, part, jnp.logical_not(first))

    for part in (A, B):
        @pl.when(jnp.logical_not(first))
        def _():
            local(out_ends, out_recv, part).wait()

        for j in range(NX):
            def came():
                dst = out_ref.at[0, pl.ds(part * HALF, HALF), head(peers[j][1])]
                pltpu.make_async_remote_copy(
                    src_ref=obuf.at[part, pl.ds(0, HALF), :], dst_ref=dst,
                    send_sem=out_send.at[j, part], recv_sem=out_recv.at[j, part],
                    device_id=(out_pipe, at(peers[j][1], y)), device_id_type=MESH).wait_recv()

            if j == 0:
                pl.when(first)(came)
            else:
                came()


def shards(queries, keys_values):
    dma = pltpu.SemaphoreType.DMA
    bf16, f32 = jnp.bfloat16, jnp.float32
    return pl.pallas_call(
        kernel,
        out_shape=jax.ShapeDtypeStruct(queries.shape, bf16),
        in_specs=[pl.BlockSpec(memory_space=pltpu.HBM), pl.BlockSpec(memory_space=pltpu.HBM)],
        out_specs=pl.BlockSpec(memory_space=pl.ANY),
        scratch_shapes=[
            pltpu.VMEM(keys_values.shape[1:], bf16),
            pltpu.VMEM((KVH, 2, 2, HALF, HD), bf16),
            pltpu.VMEM((NY, 2, 2, BLK, HD), bf16),
            pltpu.VMEM((2, BLK, WIDE), bf16),
            pltpu.VMEM((2, ROWS, HD), bf16),
            pltpu.VMEM((2, BLK, WIDE), bf16),
            pltpu.VMEM((2, ROWS, HD), f32),
            pltpu.VMEM((2, ROWS, HD), f32),
            pltpu.VMEM((2, ROWS, HD), f32),
            dma, dma((NX, 2)), dma((NX, 2)), dma((NX, 2)), dma((NX, 2)),
            dma((2, FAR)), dma((2, FAR)), dma((2, FAR)), dma((2, FAR)),
            dma((NX, 2)), dma((NX, 2)), pltpu.SemaphoreType.REGULAR,
        ],
        compiler_params=pltpu.CompilerParams(
            collective_id=0, has_side_effects=True, vmem_limit_bytes=62 * 1024 * 1024),
        cost_estimate=pl.CostEstimate(flops=3_500_000_000, bytes_accessed=4_000_000, transcendentals=3_400_000),
    )(queries, keys_values)


def solution(mesh):
    placed = (P("pipe", "ctx", None), P("pipe", "ctx", None, None))
    return jax.shard_map(
        shards, mesh=mesh, in_specs=placed, out_specs=P("pipe", "ctx", None), check_vma=False
    )
```

time: 436 us -> 47.9 us (0.11)
  the two profiles are of different devices: /device:TPU:32 before, /device:TPU:8 now
where the time goes in v2:
time: 47.9 us; the launch traced here: 47.7 us
  Pallas kernels  45.9 us (96%)
  local copies, waits for them, and re-layouts  1.77 us (4%)
    pallas_call x1, Pallas kernels, shards(): pl.pallas_call(kernel, out_shape=jax.ShapeDtypeStruct(queries.shape, bf16...  45.9 us
    unnamed x1, local copies, waits for them, and re-layouts  1.77 us

profile of v2, /device:TPU:8, one launch (start us, length us, event | category | flops | bytes accessed | tf_op | source)
XLA Modules:
  0.0 47.7 jit_solution(2994225588823641962)
XLA Ops:
  0.0 45.9 %shard_map.28 = bf16[1,128,1536]{2,1,0:T(8,128)(2,1)} custom-call(bf16[1,128,1536]{2,1,0:T(8,128)(2,1)} %q_ref.1, bf16[1,128,2,512]{3,2,1,0:T(2,128)(2,1)} %kv_ref.1), custom_call_target="tpu_custom_call" | custom-call | flops 3500000000 | bytes 4000000 | tf_op jit(solution)/shard_map/pallas_call | solution.py:313
  45.9 1.8 %copy.4 = bf16[1,128,1536]{2,1,0:T(8,128)(2,1)} copy(bf16[1,128,1536]{2,1,0:T(8,128)(2,1)} %shard_map.28) | data formatting | bytes 786432

commit v3 on v2

--- a/solution.py
+++ b/solution.py
@@ -15,9 +15,11 @@
 NX = 4
 NY = 8
 FAR = NY // 2
+CUTS = 2
 HALF = 64
 BLK = NX * HALF
 ROWS = SHARE * BLK
+CUT = BLK // CUTS
 WIDE = SHARE * HD
 GO = 2
 NEG = -1e30
@@ -63,13 +65,14 @@
     for j in range(NX):
         greet((prv, at(peers[j][0], y)))
 
-    kv_in.wait()
-    for i in range(2):
-        for part in range(2):
+    def separate(part):
+        for i in range(2):
             rows = kvin[part * HALF:(part + 1) * HALF, i, :]
             for h in range(KVH):
                 kvs[h, part, i] = rows[:, h * HD:(h + 1) * HD]
 
+    kv_in.wait()
+    separate(A)
     pl.semaphore_wait(barrier, 2 * NX + 2)
 
     def place(px, part):
@@ -135,6 +138,7 @@
             copy(j, part).wait_send()
 
     begin(kv_copy, kv_ends, kv_recv, A, first)
+    separate(B)
     begin(kv_copy, kv_ends, kv_recv, B, first)
     begin(q_copy, q_ends, q_recv, A, first)
     begin(q_copy, q_ends, q_recv, B, first)
@@ -146,11 +150,11 @@
     def owner_of(upward, d):
         return lax.rem(y + NY - d, NY) if upward else lax.rem(y + d, NY)
 
-    def ring(upward, part, d):
-        slot = kvbuf.at[owner_of(upward, d), part]
+    def ring(upward, part, d, cut):
+        slot = kvbuf.at[owner_of(upward, d), part, :, pl.ds(cut * CUT, CUT), :]
         send, recv = (up_send, up_recv) if upward else (down_send, down_recv)
         return pltpu.make_async_remote_copy(
-            src_ref=slot, dst_ref=slot, send_sem=send.at[part, d], recv_sem=recv.at[part, d],
+            src_ref=slot, dst_ref=slot, send_sem=send.at[part, d, cut], recv_sem=recv.at[part, d, cut],
             device_id=up if upward else down, device_id_type=MESH)
 
     def needed(upward, part, d):
@@ -161,24 +165,21 @@
             ok = jnp.logical_and(ok, owner + FAR - 1 >= NY if upward else owner - d - 1 >= 0)
         return ok
 
-    def pass_on(upward, part, d):
-        @pl.when(needed(upward, part, d))
-        def _():
-            ring(upward, part, d).start()
-
-    def arrive(upward, part, d):
+    def arrive(upward, part, d, cut):
         owner = owner_of(upward, d)
         ok = True if part == A else (owner + FAR - 1 >= NY if upward else y + d < NY)
-        slot = kvbuf.at[owner, part]
+        slot = kvbuf.at[owner, part, :, pl.ds(cut * CUT, CUT), :]
         send, recv = (up_send, up_recv) if upward else (down_send, down_recv)
 
         @pl.when(ok)
         def _():
             pltpu.make_async_remote_copy(
-                src_ref=slot, dst_ref=slot, send_sem=send.at[part, d - 1], recv_sem=recv.at[part, d - 1],
+                src_ref=slot, dst_ref=slot, send_sem=send.at[part, d - 1, cut], recv_sem=recv.at[part, d - 1, cut],
                 device_id=up if upward else down, device_id_type=MESH).wait_recv()
 
-        pass_on(upward, part, d)
+        @pl.when(needed(upward, part, d))
+        def _():
+            ring(upward, part, d, cut).start()
 
     last_plane = pipe == npipe - 1
 
@@ -188,21 +189,17 @@
 
     for part, j in ((A, 0), (B, 0), (A, 1), (A, 3), (A, 2), (B, 1), (B, 3), (B, 2)):
         landed(kv_copy, kv_ends, kv_recv, j, part, first)
-        piece = kvbuf.at[y, part, :, place(peers[j][1], part), :]
+        frm = peers[j][1]
+        piece = kvbuf.at[y, part, :, place(frm, part), :]
+        cut = (frm if part == A else NX - 1 - frm) // (NX // CUTS)
         for upward in (True, False):
             @pl.when(needed(upward, part, 0))
             def _():
                 pltpu.make_async_remote_copy(
                     src_ref=piece, dst_ref=piece,
-                    send_sem=(up_send if upward else down_send).at[part, 0],
-                    recv_sem=(up_recv if upward else down_recv).at[part, 0],
+                    send_sem=(up_send if upward else down_send).at[part, 0, cut],
+                    recv_sem=(up_recv if upward else down_recv).at[part, 0, cut],
                     device_id=up if upward else down, device_id_type=MESH).start()
-
-    for part in (A, B):
-        for j in range(NX):
-            landed(q_copy, q_ends, q_recv, j, part, first)
-        for g in range(SHARE):
-            qs[part, g * BLK:(g + 1) * BLK, :] = qbuf[part, :, g * HD:(g + 1) * HD]
 
     factor = math.log2(math.e) / math.sqrt(HD)
 
@@ -223,36 +220,48 @@
         total[rows] = total[rows] * fade + jnp.sum(w, axis=1, keepdims=True)
         acc[rows] = acc[rows] * fade + jnp.dot(w.astype(jnp.bfloat16), values, preferred_element_type=jnp.float32)
 
-    attend(A, [(y, A)], 0)
-    attend(B, [(y, A), (y, B)], BLK)
-
     def same(d):
         for upward in (True, False):
             owner = owner_of(upward, d)
             part = jnp.where(owner < y, A, B)
             attend(part, [(owner, part)])
 
+    def late(d):
+        attend(B, [(owner_of(True, d), A), (owner_of(False, d), A)])
+
+    def both(part, d):
+        for cut in range(CUTS):
+            arrive(True, part, d, cut)
+            arrive(False, part, d, cut)
+
+        @pl.when(jnp.logical_and(jnp.logical_and(d == GO, part == B), jnp.logical_and(last_plane, first)))
+        def _():
+            pl.semaphore_signal(go, inc=1, device_id=twin, device_id_type=MESH)
+
+    both(A, 1)
+    both(B, 1)
+
+    for part in (A, B):
+        for j in range(NX):
+            landed(q_copy, q_ends, q_recv, j, part, first)
+        for g in range(SHARE):
+            qs[part, g * BLK:(g + 1) * BLK, :] = qbuf[part, :, g * HD:(g + 1) * HD]
+
+    attend(A, [(y, A)], 0)
+    attend(B, [(y, A), (y, B)], BLK)
+
     def step(d, _):
-        arrive(True, A, d)
-        arrive(False, A, d)
-
-        @pl.when(d > 1)
-        def _():
-            same(d - 1)
-
-        arrive(True, B, d)
-        arrive(False, B, d)
-
-        @pl.when(jnp.logical_and(d == GO, jnp.logical_and(last_plane, first)))
-        def _():
-            pl.semaphore_signal(go, inc=1, device_id=twin, device_id_type=MESH)
-
-        attend(B, [(owner_of(True, d), A), (owner_of(False, d), A)])
+        both(A, d)
+        late(d - 1)
+        both(B, d)
+        same(d - 1)
         return 0
 
-    lax.fori_loop(1, FAR, step, 0)
+    lax.fori_loop(2, FAR, step, 0)
+    late(FAR - 1)
     same(FAR - 1)
-    arrive(True, A, FAR)
+    for cut in range(CUTS):
+        arrive(True, A, FAR, cut)
     far = owner_of(True, FAR)
 
     @pl.when(far < y)
@@ -266,7 +275,8 @@
         begin(out_copy, out_ends, out_recv, part, jnp.logical_not(first))
 
     finish(A)
-    arrive(False, B, FAR)
+    for cut in range(CUTS):
+        arrive(False, B, FAR, cut)
 
     @pl.when(far < y)
     def _():
@@ -285,7 +295,8 @@
             for upward in (True, False):
                 @pl.when(needed(upward, part, d))
                 def _():
-                    ring(upward, part, d).wait_send()
+                    for cut in range(CUTS):
+                        ring(upward, part, d, cut).wait_send()
         sent(out_copy, part, jnp.logical_not(first))
 
     for part in (A, B):
@@ -312,7 +323,7 @@
     bf16, f32 = jnp.bfloat16, jnp.float32
     return pl.pallas_call(
         kernel,
-        out_shape=jax.ShapeDtypeStruct(queries.shape, bf16),
+        out_shape=pltpu.VMEM(queries.shape, bf16),
         in_specs=[pl.BlockSpec(memory_space=pltpu.HBM), pl.BlockSpec(memory_space=pltpu.HBM)],
         out_specs=pl.BlockSpec(memory_space=pl.ANY),
         scratch_shapes=[
@@ -326,13 +337,13 @@
             pltpu.VMEM((2, ROWS, HD), f32),
             pltpu.VMEM((2, ROWS, HD), f32),
             dma, dma((NX, 2)), dma((NX, 2)), dma((NX, 2)), dma((NX, 2)),
-            dma((2, FAR)), dma((2, FAR)), dma((2, FAR)), dma((2, FAR)),
+            dma((2, FAR, CUTS)), dma((2, FAR, CUTS)), dma((2, FAR, CUTS)), dma((2, FAR, CUTS)),
             dma((NX, 2)), dma((NX, 2)), pltpu.SemaphoreType.REGULAR,
         ],
         compiler_params=pltpu.CompilerParams(
-            collective_id=0, has_side_effects=True, vmem_limit_bytes=62 * 1024 * 1024),
+            collective_id=0, has_side_effects=True, vmem_limit_bytes=48 * 1024 * 1024),
         cost_estimate=pl.CostEstimate(flops=3_500_000_000, bytes_accessed=4_000_000, transcendentals=3_400_000),
-    )(queries, keys_values)
+    )(pltpu.with_memory_space_constraint(queries, pltpu.HBM), pltpu.with_memory_space_constraint(keys_values, pltpu.HBM))
 
 
 def solution(mesh):

time: 47.9 us -> 43 us (0.90)
  Pallas kernels: 45.9 us -> 42.1 us
  local copies, waits for them, and re-layouts: 1.77 us -> 0.75 us
    pallas_call x1, Pallas kernels: 45.9 us -> 42.1 us  [shards(): pl.pallas_call(kernel, out_shape=pltpu.VMEM(queries.shape, bf16), in_spec...]
    unnamed x1, local copies, waits for them, and re-layouts: 1.77 us -> 0.75 us
where the time goes in v3:
time: 43 us; the launch traced here: 42.8 us
  Pallas kernels  42.1 us (98%)
  local copies, waits for them, and re-layouts  0.75 us (2%)
    pallas_call x1, Pallas kernels, shards(): pl.pallas_call(kernel, out_shape=pltpu.VMEM(queries.shape, bf16), in_spec...  42.1 us

profile of v3, /device:TPU:8, one launch (start us, length us, event | category | flops | bytes accessed | tf_op | source)
XLA Modules:
  0.0 42.8 jit_solution(14513955941051176149)
XLA Ops:
  0.0 42.1 %shard_map.28 = bf16[1,128,1536]{2,1,0:T(8,128)(2,1)S(1)} custom-call(bf16[1,128,1536]{2,1,0:T(8,128)(2,1)} %q_ref.1, bf16[1,128,2,512]{3,2,1,0:T(2,128)(2,1)} %kv_ref.1), custom_call_target="tpu_custom_call" | custom-call | flops 3500000000 | bytes 4000000 | tf_op jit(solution)/shard_map/pallas_call | solution.py:324
  42.1 0.7 %copy.4 = bf16[1,128,1536]{2,1,0:T(8,128)(2,1)} copy(bf16[1,128,1536]{2,1,0:T(8,128)(2,1)S(1)} %shard_map.28) | data formatting | bytes 786432

commit v4 on v3

--- a/solution.py
+++ b/solution.py
@@ -157,21 +157,22 @@
             src_ref=slot, dst_ref=slot, send_sem=send.at[part, d, cut], recv_sem=recv.at[part, d, cut],
             device_id=up if upward else down, device_id_type=MESH)
 
+    def travels(upward, part, owner, d):
+        if part == A:
+            return d <= (FAR if upward else FAR - 1)
+        if upward:
+            return jnp.logical_and(owner > FAR, d <= FAR)
+        return jnp.logical_and(owner >= d, d <= jnp.where(owner == FAR, FAR, FAR - 1))
+
     def needed(upward, part, d):
-        hops = FAR if upward == (part == A) else FAR - 1
-        ok = d < hops
-        if part == B:
-            owner = owner_of(upward, d)
-            ok = jnp.logical_and(ok, owner + FAR - 1 >= NY if upward else owner - d - 1 >= 0)
-        return ok
+        return travels(upward, part, owner_of(upward, d), d + 1)
 
     def arrive(upward, part, d, cut):
         owner = owner_of(upward, d)
-        ok = True if part == A else (owner + FAR - 1 >= NY if upward else y + d < NY)
         slot = kvbuf.at[owner, part, :, pl.ds(cut * CUT, CUT), :]
         send, recv = (up_send, up_recv) if upward else (down_send, down_recv)
 
-        @pl.when(ok)
+        @pl.when(travels(upward, part, owner, d))
         def _():
             pltpu.make_async_remote_copy(
                 src_ref=slot, dst_ref=slot, send_sem=send.at[part, d - 1, cut], recv_sem=recv.at[part, d - 1, cut],
@@ -231,8 +232,8 @@
 
     def both(part, d):
         for cut in range(CUTS):
+            arrive(False, part, d, cut)
             arrive(True, part, d, cut)
-            arrive(False, part, d, cut)
 
         @pl.when(jnp.logical_and(jnp.logical_and(d == GO, part == B), jnp.logical_and(last_plane, first)))
         def _():
@@ -276,6 +277,7 @@
 
     finish(A)
     for cut in range(CUTS):
+        arrive(True, B, FAR, cut)
         arrive(False, B, FAR, cut)
 
     @pl.when(far < y)

time: 43 us -> 42.5 us (0.988)
  Pallas kernels: 42.1 us -> 41.6 us
    pallas_call x1, Pallas kernels: 42.1 us -> 41.6 us  [shards(): pl.pallas_call(kernel, out_shape=pltpu.VMEM(queries.shape, bf16), in_spec...]
where the time goes in v4:
time: 42.5 us; the launch traced here: 42.3 us
  Pallas kernels  41.6 us (98%)
  local copies, waits for them, and re-layouts  0.75 us (2%)
    pallas_call x1, Pallas kernels, shards(): pl.pallas_call(kernel, out_shape=pltpu.VMEM(queries.shape, bf16), in_spec...  41.6 us

profile of v4, /device:TPU:8, one launch (start us, length us, event | category | flops | bytes accessed | tf_op | source)
XLA Modules:
  0.0 42.3 jit_solution(1820448838734022255)
XLA Ops:
  0.0 41.6 %shard_map.28 = bf16[1,128,1536]{2,1,0:T(8,128)(2,1)S(1)} custom-call(bf16[1,128,1536]{2,1,0:T(8,128)(2,1)} %q_ref.1, bf16[1,128,2,512]{3,2,1,0:T(2,128)(2,1)} %kv_ref.1), custom_call_target="tpu_custom_call" | custom-call | flops 3500000000 | bytes 4000000 | tf_op jit(solution)/shard_map/pallas_call | solution.py:326
  41.6 0.7 %copy.4 = bf16[1,128,1536]{2,1,0:T(8,128)(2,1)} copy(bf16[1,128,1536]{2,1,0:T(8,128)(2,1)S(1)} %shard_map.28) | data formatting | bytes 786432

commit v5 on v4

--- a/solution.py
+++ b/solution.py
@@ -276,17 +276,14 @@
         begin(out_copy, out_ends, out_recv, part, jnp.logical_not(first))
 
     finish(A)
+    attend(B, [(far, A)])
     for cut in range(CUTS):
+        arrive(False, B, FAR, cut)
         arrive(True, B, FAR, cut)
-        arrive(False, B, FAR, cut)
-
-    @pl.when(far < y)
-    def _():
-        attend(B, [(far, A)])
 
     @pl.when(far > y)
     def _():
-        attend(B, [(far, A), (far, B)])
+        attend(B, [(far, B)])
 
     finish(B)
 

time: 42.5 us -> 42.3 us (level)
  no operation moved by 1% of the time
where the time goes in v5:
time: 42.3 us; the launch traced here: 42.2 us
  Pallas kernels  41.4 us (98%)
  local copies, waits for them, and re-layouts  0.75 us (2%)
    pallas_call x1, Pallas kernels, shards(): pl.pallas_call(kernel, out_shape=pltpu.VMEM(queries.shape, bf16), in_spec...  41.4 us

profile of v5, /device:TPU:8, one launch (start us, length us, event | category | flops | bytes accessed | tf_op | source)
XLA Modules:
  0.0 42.2 jit_solution(1753889431358568981)
XLA Ops:
  0.0 41.4 %shard_map.28 = bf16[1,128,1536]{2,1,0:T(8,128)(2,1)S(1)} custom-call(bf16[1,128,1536]{2,1,0:T(8,128)(2,1)} %q_ref.1, bf16[1,128,2,512]{3,2,1,0:T(2,128)(2,1)} %kv_ref.1), custom_call_target="tpu_custom_call" | custom-call | flops 3500000000 | bytes 4000000 | tf_op jit(solution)/shard_map/pallas_call | solution.py:323
  41.4 0.7 %copy.4 = bf16[1,128,1536]{2,1,0:T(8,128)(2,1)} copy(bf16[1,128,1536]{2,1,0:T(8,128)(2,1)S(1)} %shard_map.28) | data formatting | bytes 786432

commit v6 on v5

--- a/solution.py
+++ b/solution.py
@@ -104,7 +104,7 @@
     q_copy = lambda j, part: remote(q_ends, q_send, q_recv, j, part, in_pipe)
     out_copy = lambda j, part: remote(out_ends, out_send, out_recv, j, part, out_pipe)
 
-    def begin(copy, ends, recv, part, stays):
+    def begin(copy, ends, recv, part, stays, order=(1, 3, 2)):
         @pl.when(stays)
         def _():
             local(ends, recv, part).start()
@@ -113,7 +113,7 @@
         def _():
             copy(0, part).start()
 
-        for j in (1, 3, 2):
+        for j in order:
             copy(j, part).start()
 
     def landed(copy, ends, recv, j, part, stays):
@@ -273,7 +273,7 @@
         o = acc[part] / total[part]
         for g in range(SHARE):
             obuf[part, :, g * HD:(g + 1) * HD] = o[g * BLK:(g + 1) * BLK].astype(jnp.bfloat16)
-        begin(out_copy, out_ends, out_recv, part, jnp.logical_not(first))
+        begin(out_copy, out_ends, out_recv, part, jnp.logical_not(first), (2, 1, 3))
 
     finish(A)
     attend(B, [(far, A)])

time: 42.3 us -> 42.1 us (level)
  no operation moved by 1% of the time
where the time goes in v6:
time: 42.1 us; the launch traced here: 41.9 us
  Pallas kernels  41.2 us (98%)
  local copies, waits for them, and re-layouts  0.75 us (2%)
    pallas_call x1, Pallas kernels, shards(): pl.pallas_call(kernel, out_shape=pltpu.VMEM(queries.shape, bf16), in_spec...  41.2 us

profile of v6, /device:TPU:8, one launch (start us, length us, event | category | flops | bytes accessed | tf_op | source)
XLA Modules:
  0.0 41.9 jit_solution(5526371808519811279)
XLA Ops:
  0.0 41.2 %shard_map.28 = bf16[1,128,1536]{2,1,0:T(8,128)(2,1)S(1)} custom-call(bf16[1,128,1536]{2,1,0:T(8,128)(2,1)} %q_ref.1, bf16[1,128,2,512]{3,2,1,0:T(2,128)(2,1)} %kv_ref.1), custom_call_target="tpu_custom_call" | custom-call | flops 3500000000 | bytes 4000000 | tf_op jit(solution)/shard_map/pallas_call | solution.py:323
  41.2 0.7 %copy.4 = bf16[1,128,1536]{2,1,0:T(8,128)(2,1)} copy(bf16[1,128,1536]{2,1,0:T(8,128)(2,1)S(1)} %shard_map.28) | data formatting | bytes 786432
